TPU v7x, 128 devices: a whole 4x4x4 slice. The times are simulated.
128 devices in a mesh: sec: 8 (over x, core), op: 16 (over y, z).
Axes of the slice: x: 4, y: 4, z: 4, core: 2. Of those that a mesh axis runs over, the one named last changes fastest.
Arguments:
- psi: bfloat16 [8192, 256], P(('sec', 'op')), may hold values from -6 to 6
- left_env: bfloat16 [384, 32, 256, 256], P('op', 'sec'), may hold values from -0.01953125 to 0.01953125
- right_env: bfloat16 [384, 32, 256, 256], P('op', 'sec'), may hold values from -0.375 to 0.375
- term_src: int32 [384, 32], P('op', 'sec'), may hold values from 0 to 31, as said below
- block_dims: int32 [2, 32], replicated, may hold values from 64 to 256, as said below
Outputs:
- sigma: bfloat16 [8192, 256], P(('sec', 'op'))
Inputs may be any that keep to these rules, and one draw needn't show every extreme that they name: |term_src[t, k] - k| <= 2 for every t and k, and term_src[t, k] = k + 2 for some t and k. `block_dims`: every entry is a multiple of 4; 256 is reached in each row.
All inputs are finite; a program needn't handle non-finite values.
Results may differ from a plain program's by a relative error of at most 0.0049.
Values may be sent and summed in bfloat16 or wider, within the bound.
A program may use at most 128 MiB of HBM per device.

v0:
```python
import jax
import jax.numpy as jnp
from jax import lax
from jax.sharding import PartitionSpec as P


def padded(cells, sides, width):
    for axis, dim in sides:
        count = lax.axis_size(axis)
        ends = count - 1
        head = lax.slice_in_dim(cells, 0, width, axis=dim)
        tail = lax.slice_in_dim(cells, cells.shape[dim] - width, cells.shape[dim], axis=dim)
        cells = jnp.concatenate(
            [
                lax.ppermute(tail, axis, [(i, (i + 1) % count) for i in range(ends)]),
                cells,
                lax.ppermute(head, axis, [((i + 1) % count, i) for i in range(ends)]),
            ],
            axis=dim,
        )
    return cells


def lookup_dims(block_ids, block_dims):
    count = block_dims.shape[1]
    every_id = jnp.arange(count, dtype=jnp.int32)
    match = block_ids[..., None] == every_id
    rows_used = jnp.sum(jnp.where(match, block_dims[0], 0), axis=-1)
    cols_used = jnp.sum(jnp.where(match, block_dims[1], 0), axis=-1)
    return (rows_used, cols_used)


def shards(psi, left_env, right_env, term_src, block_dims):
    side = psi.shape[1]
    per_sec = left_env.shape[1]
    local_rows = psi.shape[0]
    group_size = lax.axis_size("op")
    extended = padded(psi, (("sec", 0),), local_rows)
    gathered = lax.all_gather(extended, "op", axis=0, tiled=True)
    arranged = gathered.reshape(group_size, 3, local_rows, side).transpose(1, 0, 2, 3)
    blocks = arranged.reshape(-1, side, side)
    first_block = lax.axis_index("sec") * per_sec - per_sec
    local_src = term_src - first_block
    selected = jnp.take(blocks, local_src, axis=0)
    places = jnp.arange(side, dtype=jnp.int32)
    rows_used, cols_used = lookup_dims(term_src, block_dims)
    keep = (places[:, None] < rows_used[..., None, None]) & (
        places[None, :] < cols_used[..., None, None]
    )
    masked = jnp.where(keep, selected, jnp.zeros_like(selected))
    half = jnp.einsum(
        "tkij,tkjl->tkil", masked, right_env, preferred_element_type=jnp.float32
    ).astype(jnp.bfloat16)
    partial_value = jnp.einsum("tkij,tkjl->kil", left_env, half, preferred_element_type=jnp.float32)
    partial_value = partial_value.reshape(per_sec * side, side)
    summed = lax.psum_scatter(partial_value, "op", scatter_dimension=0, tiled=True)
    row_start = (lax.axis_index("sec") * group_size + lax.axis_index("op")) * local_rows
    global_rows = row_start + jnp.arange(local_rows, dtype=jnp.int32)
    out_blocks = global_rows // side
    inner_rows = global_rows % side
    out_rows_used, out_cols_used = lookup_dims(out_blocks, block_dims)
    out_keep = (inner_rows < out_rows_used)[:, None] & (places[None, :] < out_cols_used[:, None])
    return jnp.where(out_keep, summed, jnp.zeros_like(summed)).astype(jnp.bfloat16)


def solution(mesh):
    placed = (
        P(("sec", "op"), None),
        P("op", "sec", None, None),
        P("op", "sec", None, None),
        P("op", "sec"),
        P(),
    )
    return jax.shard_map(
        shards, mesh=mesh, in_specs=placed, out_specs=P(("sec", "op"), None), check_vma=False
    )
```

profile of v0, /device:TPU:0, one launch (start us, length us, event | category | flops | bytes accessed | tf_op | source)
XLA Modules:
  0.0 178.6 jit_solution(1798577908962675282)
XLA Ops:
  6.5 0.0 all-gather.2.cloned.1.call-start
  6.5 1.3 collective-permute-start
  7.8 1.3 collective-permute-start.1
  9.1 0.0 collective-permute-done
  9.1 3.8 %collective-permute-done.1 = bf16[64,256]{1,0:T(8,128)(2,1)S(1)} collective-permute-done((bf16[64,256]{1,0:T(8,128)(2,1)}, bf16[64,256]{1,0:T(8,128)(2,1)S(1)}, u32[]{:S(2)}, u32[]{:S(2)}) %collective-permute-start.1) | collective-permute-done | bytes 32800 | tf_op jit(solution)/shard_map/ppermute | solution.py:17
  12.9 1.4 pad_maximum_fusion
  14.3 0.0 all-gather.2.cloned.1.call-update
  14.4 0.0 reduce-scatter.2.cloned.1.call-start
  14.4 0.7 compare_and_fusion
  15.1 0.1 copy.21
  15.2 0.1 reshape.72
  15.3 0.8 slice_bitcast_fusion
  16.1 1.0 select_reduce_fusion.1
  17.0 0.1 iota_compare_fusion
  17.1 45.8 %all-gather.2.cloned.1.call-done = bf16[3072,256]{1,0:T(8,128)(2,1)} async-done(((bf16[192,256]{1,0:T(8,128)(2,1)}), bf16[3072,256]{1,0:T(8,128)(2,1)}) %all-gather.2.cloned.1.call-update) | async-done | bytes 1572880 | tf_op jit(solution)/shard_map/all_gather | solution.py:39
  63.0 1.5 copy.20
  64.5 6.7 %gather_fusion = bf16[96,256,256]{2,1,0:T(8,128)(2,1)} fusion(bf16[12,256,256]{2,1,0:T(8,128)(2,1)S(1)} %bitcast.16, s32[1024]{0:T(1024)S(1)} %pad_clamp_fusion), kind=kCustom, calls=%fused_computation | custom fusion | bytes 25166208 | tf_op jit(solution)/shard_map/jit(_take)/gather | solution.py:44
  71.2 13.9 %fusion.26 = bf16[24,4,256,256]{3,2,0,1:T(8,128)(2,1)} fusion(bf16[24,4,256,256]{3,2,1,0:T(8,128)(2,1)} %param.7, bf16[24,4,256,256]{3,2,1,0:T(8,128)(2,1)} %bitcast.17, pred[24,4]{0,1:T(4,128)(4,1)S(1)} %get-tuple-element.9, pred[24,4,256]{2,0,1:T(8,128)(4,1)S(1)} %get-tuple-element.13, pred[24,4,256]{2,0,1:T(8,128)(4,1)S(1)} %get-tuple-element.14), kind=kOutput, calls=%fused_computation.7.clone.1 | convolution fusion | flops 3246391296 | bytes 37797984 | tf_op jit(solution)/shard_map/tkij,tkjl->tkil/dot_general | solution.py:51
  85.1 12.6 %fusion.1 = f32[4,256,256,1]{1,2,3,0:T(8,128)} fusion(bf16[24,4,256,256]{3,2,1,0:T(8,128)(2,1)} %param.6, bf16[24,4,256,256]{3,2,0,1:T(8,128)(2,1)} %fusion.26), kind=kOutput, calls=%fused_computation.3 | convolution fusion | flops 3221225472 | bytes 26214400 | tf_op jit(solution)/shard_map/tkij,tkjl->kil/dot_general | solution.py:54
  97.7 0.0 reduce-scatter.2.cloned.1.call-update
  97.8 0.1 select_reduce_fusion.3
  97.9 72.4 %reduce-scatter.2.cloned.1.call-done = f32[64,256]{1,0:T(8,128)} async-done(((f32[1024,256]{1,0:T(8,128)}), f32[64,256]{1,0:T(8,128)}) %reduce-scatter.2.cloned.1.call-update) | async-done | bytes 65552 | tf_op jit(solution)/shard_map/reduce_scatter | solution.py:56
  170.2 1.5 select_convert_fusion
  (3 shorter events, 0.0 us)
Async XLA Ops:
  6.5 56.4 %all-gather.2.cloned.1.call-start = ((), (), s32[]{:S(2)}) async-start(), calls=%async_computation.1 | async-start | bytes 1671168 | tf_op jit(solution)/shard_map/all_gather | solution.py:39
  6.5 2.6 %collective-permute-start = (bf16[64,256]{1,0:T(8,128)(2,1)}, bf16[64,256]{1,0:T(8,128)(2,1)S(1)}, u32[]{:S(2)}, u32[]{:S(2)}) collective-permute-start(bf16[64,256]{1,0:T(8,128)(2,1)} %param.5), channel_id=1, source_target_pairs={{0,16},{16,32},{32,48},{48,64},{64,80},{80,96},{96,112},{1,17},{17... | collective-permute-start | bytes 98312 | tf_op jit(solution)/shard_map/ppermute | solution.py:15
  7.8 5.1 %collective-permute-start.1 = (bf16[64,256]{1,0:T(8,128)(2,1)}, bf16[64,256]{1,0:T(8,128)(2,1)S(1)}, u32[]{:S(2)}, u32[]{:S(2)}) collective-permute-start(bf16[64,256]{1,0:T(8,128)(2,1)} %param.5), channel_id=1, source_target_pairs={{16,0},{32,16},{48,32},{64,48},{80,64},{96,80},{112,96},{17,1},{33... | collective-permute-start | bytes 98312 | tf_op jit(solution)/shard_map/ppermute | solution.py:17
  14.4 155.9 %reduce-scatter.2.cloned.1.call-start = ((), (), s32[]{:S(2)}) async-start(), calls=%async_computation.2 | async-start | bytes 1114112 | tf_op jit(solution)/shard_map/reduce_scatter | solution.py:56
Sparse Core Ops, SparseCore 0:
  14.5 48.4 all-gather.1
  97.8 72.3 reduce-scatter.1
where the time goes:
time: 179 us
  waiting for transfers between devices  122 us (68%)
  matrix products  26.5 us (15%)
  between operations  13.5 us (8%)
  local copies, waits for them, and re-layouts  9.16 us (5%)
  other arithmetic  4.82 us (3%)
  starting transfers between devices  2.62 us (1%)
    reduce_scatter x1, waiting for transfers between devices, shards(): lax.psum_scatter(partial_value, 'op', scatter_dimension=0, tiled=True)  72.4 us
    all_gather x1, waiting for transfers between devices, shards(): gathered = lax.all_gather(extended, 'op', axis=0, tiled=True)  45.8 us
    dot_general x1, matrix products, shards(): jnp.einsum('tkij,tkjl->tkil', masked, right_env, preferred_element_type=j...  13.9 us
    dot_general x1, matrix products, shards(): jnp.einsum('tkij,tkjl->kil', left_env, half, preferred_element_type=jnp.f...  12.6 us
    gather x1, local copies, waits for them, and re-layouts, shards(): selected = jnp.take(blocks, local_src, axis=0)  6.71 us
    ppermute x1, waiting for transfers between devices, padded(): lax.ppermute(head, axis, [((i + 1) % count, i) for i in range(ends)])  3.81 us
  transfers between devices with their start and end apart: 4, of which 3 were waited for; matrix products, arithmetic and copies ran while one was open for 2% of the time, Pallas kernels for 0%

commit v1 on v0

--- a/solution.py
+++ b/solution.py
@@ -36,7 +36,9 @@
     local_rows = psi.shape[0]
     group_size = lax.axis_size("op")
     extended = padded(psi, (("sec", 0),), local_rows)
-    gathered = lax.all_gather(extended, "op", axis=0, tiled=True)
+    gathered = jnp.concatenate(
+        lax.all_to_all(jnp.stack([extended] * lax.axis_size("op")), "op", 0, 0), axis=0
+    )
     arranged = gathered.reshape(group_size, 3, local_rows, side).transpose(1, 0, 2, 3)
     blocks = arranged.reshape(-1, side, side)
     first_block = lax.axis_index("sec") * per_sec - per_sec

time: 179 us -> 164 us (0.916)
  waiting for transfers between devices: 122 us -> 100 us
  starting transfers between devices: 2.62 us -> 10.7 us
    all_gather x1 -> x0, waiting for transfers between devices: 45.8 us -> none  [shards(): gathered = lax.all_gather(extended, 'op', axis=0, tiled=True)]
    all_to_all x0 -> x1, waiting for transfers between devices: none -> 19.1 us  [shards(): lax.all_to_all(jnp.stack([extended] * lax.axis_size('op')), 'op', 0, 0)]
    all_to_all x0 -> x1, starting transfers between devices: none -> 8.05 us  [shards(): lax.all_to_all(jnp.stack([extended] * lax.axis_size('op')), 'op', 0, 0)]
    reduce_scatter x1, waiting for transfers between devices: 72.4 us -> 77.1 us  [shards(): lax.psum_scatter(partial_value, 'op', scatter_dimension=0, tiled=True)]
where the time goes in v1:
time: 164 us
  waiting for transfers between devices  100 us (61%)
  matrix products  26.5 us (16%)
  between operations  13.5 us (8%)
  starting transfers between devices  10.7 us (7%)
  local copies, waits for them, and re-layouts  9.06 us (6%)
  other arithmetic  4.19 us (3%)
    reduce_scatter x1, waiting for transfers between devices, shards(): lax.psum_scatter(partial_value, 'op', scatter_dimension=0, tiled=True)  77.1 us
    all_to_all x1, waiting for transfers between devices, shards(): lax.all_to_all(jnp.stack([extended] * lax.axis_size('op')), 'op', 0, 0)  19.1 us
    dot_general x1, matrix products, shards(): jnp.einsum('tkij,tkjl->tkil', masked, right_env, preferred_element_type=j...  13.9 us
    dot_general x1, matrix products, shards(): jnp.einsum('tkij,tkjl->kil', left_env, half, preferred_element_type=jnp.f...  12.6 us
    all_to_all x1, starting transfers between devices, shards(): lax.all_to_all(jnp.stack([extended] * lax.axis_size('op')), 'op', 0, 0)  8.05 us
    gather x1, local copies, waits for them, and re-layouts, shards(): selected = jnp.take(blocks, local_src, axis=0)  6.71 us
    ppermute x1, waiting for transfers between devices, padded(): lax.ppermute(head, axis, [((i + 1) % count, i) for i in range(ends)])  3.81 us
  transfers between devices with their start and end apart: 4, of which 3 were waited for; matrix products, arithmetic and copies ran while one was open for 2% of the time, Pallas kernels for 0%

profile of v1, /device:TPU:0, one launch (start us, length us, event | category | flops | bytes accessed | tf_op | source)
XLA Modules:
  0.0 163.9 jit_solution(12191976829752989103)
XLA Ops:
  6.5 1.3 collective-permute-start
  7.8 1.3 collective-permute-start.1
  9.1 0.0 collective-permute-done
  9.1 3.8 %collective-permute-done.1 = bf16[64,256]{1,0:T(8,128)(2,1)S(1)} collective-permute-done((bf16[64,256]{1,0:T(8,128)(2,1)}, bf16[64,256]{1,0:T(8,128)(2,1)S(1)}, u32[]{:S(2)}, u32[]{:S(2)}) %collective-permute-start.1) | collective-permute-done | bytes 32800 | tf_op jit(solution)/shard_map/ppermute | solution.py:17
  12.9 0.8 pad_maximum_fusion
  13.7 1.3 stack.2
  15.0 8.0 %all-to-all-start = ((bf16[16,192,256]{2,1,0:T(8,128)(2,1)}), bf16[16,192,256]{2,1,0:T(8,128)(2,1)S(1)}, u32[]{:S(2)}, u32[]{:S(2)}) async-start(bf16[16,192,256]{2,1,0:T(8,128)(2,1)} %stack.2), calls=%async_computation | async-start | bytes 3145728 | tf_op jit(solution)/shard_map/all_to_all | solution.py:40
  23.1 0.0 reduce-scatter.2.cloned.1.call-start
  23.1 0.7 compare_and_fusion
  23.8 0.1 copy.21
  23.9 0.1 reshape.70
  24.0 0.8 slice_bitcast_fusion
  24.8 1.0 select_reduce_fusion.1
  25.7 0.1 iota_compare_fusion
  25.9 19.1 %all-to-all-done = bf16[16,192,256]{2,1,0:T(8,128)(2,1)S(1)} async-done(((bf16[16,192,256]{2,1,0:T(8,128)(2,1)}), bf16[16,192,256]{2,1,0:T(8,128)(2,1)S(1)}, u32[]{:S(2)}, u32[]{:S(2)}) %all-to-all-start) | async-done | bytes 1572896 | tf_op jit(solution)/shard_map/all_to_all | solution.py:40
  44.9 0.1 copy.20
  45.0 6.7 %gather_fusion = bf16[96,256,256]{2,1,0:T(8,128)(2,1)} fusion(bf16[12,256,256]{2,1,0:T(8,128)(2,1)S(1)} %bitcast.16, s32[1024]{0:T(1024)S(1)} %pad_clamp_fusion), kind=kCustom, calls=%fused_computation | custom fusion | bytes 25166208 | tf_op jit(solution)/shard_map/jit(_take)/gather | solution.py:46
  51.7 13.9 %fusion.26 = bf16[24,4,256,256]{3,2,0,1:T(8,128)(2,1)} fusion(bf16[24,4,256,256]{3,2,1,0:T(8,128)(2,1)} %param.7, bf16[24,4,256,256]{3,2,1,0:T(8,128)(2,1)} %bitcast.17, pred[24,4]{0,1:T(4,128)(4,1)S(1)} %get-tuple-element.9, pred[24,4,256]{2,0,1:T(8,128)(4,1)S(1)} %get-tuple-element.13, pred[24,4,256]{2,0,1:T(8,128)(4,1)S(1)} %get-tuple-element.14), kind=kOutput, calls=%fused_computation.7.clone.1 | convolution fusion | flops 3246391296 | bytes 37797984 | tf_op jit(solution)/shard_map/tkij,tkjl->tkil/dot_general | solution.py:53
  65.6 12.6 %fusion.1 = f32[4,256,256,1]{1,2,3,0:T(8,128)} fusion(bf16[24,4,256,256]{3,2,1,0:T(8,128)(2,1)} %param.6, bf16[24,4,256,256]{3,2,0,1:T(8,128)(2,1)} %fusion.26), kind=kOutput, calls=%fused_computation.3 | convolution fusion | flops 3221225472 | bytes 26214400 | tf_op jit(solution)/shard_map/tkij,tkjl->kil/dot_general | solution.py:56
  78.3 0.0 reduce-scatter.2.cloned.1.call-update
  78.3 0.1 select_reduce_fusion.3
  78.4 77.1 %reduce-scatter.2.cloned.1.call-done = f32[64,256]{1,0:T(8,128)} async-done(((f32[1024,256]{1,0:T(8,128)}), f32[64,256]{1,0:T(8,128)}) %reduce-scatter.2.cloned.1.call-update) | async-done | bytes 65552 | tf_op jit(solution)/shard_map/reduce_scatter | solution.py:58
  155.5 1.5 select_convert_fusion
  (3 shorter events, 0.0 us)
Async XLA Ops:
  6.5 2.6 %collective-permute-start = (bf16[64,256]{1,0:T(8,128)(2,1)}, bf16[64,256]{1,0:T(8,128)(2,1)S(1)}, u32[]{:S(2)}, u32[]{:S(2)}) collective-permute-start(bf16[64,256]{1,0:T(8,128)(2,1)} %param.5), channel_id=1, source_target_pairs={{0,16},{16,32},{32,48},{48,64},{64,80},{80,96},{96,112},{1,17},{17... | collective-permute-start | bytes 98312 | tf_op jit(solution)/shard_map/ppermute | solution.py:15
  7.8 5.1 %collective-permute-start.1 = (bf16[64,256]{1,0:T(8,128)(2,1)}, bf16[64,256]{1,0:T(8,128)(2,1)S(1)}, u32[]{:S(2)}, u32[]{:S(2)}) collective-permute-start(bf16[64,256]{1,0:T(8,128)(2,1)} %param.5), channel_id=1, source_target_pairs={{16,0},{32,16},{48,32},{64,48},{80,64},{96,80},{112,96},{17,1},{33... | collective-permute-start | bytes 98312 | tf_op jit(solution)/shard_map/ppermute | solution.py:17
  15.0 29.9 %all-to-all-start = ((bf16[16,192,256]{2,1,0:T(8,128)(2,1)}), bf16[16,192,256]{2,1,0:T(8,128)(2,1)S(1)}, u32[]{:S(2)}, u32[]{:S(2)}) async-start(bf16[16,192,256]{2,1,0:T(8,128)(2,1)} %stack.2), calls=%async_computation | async-start | bytes 3145728 | tf_op jit(solution)/shard_map/all_to_all | solution.py:40
  23.1 132.4 %reduce-scatter.2.cloned.1.call-start = ((), (), s32[]{:S(2)}) async-start(), calls=%async_computation.2 | async-start | bytes 1114112 | tf_op jit(solution)/shard_map/reduce_scatter | solution.py:58
Sparse Core Ops, SparseCore 0:
  78.4 77.0 reduce-scatter.1
